TPU v7x, 32 devices: a whole 2x2x4 slice. The times are simulated.
32 devices in a mesh: blk: 4 (over z), grp: 8 (over y, x, core).
Axes of the slice: x: 2, y: 2, z: 4, core: 2. Of those that a mesh axis runs over, the one named last changes fastest.
Arguments:
- obj_query: bfloat16 [2048, 1536], P(('blk', 'grp')), may hold values from -64 to 64
- grad_out: bfloat16 [2048, 1536], P(('blk', 'grp')), may hold values from -256 to 256
- pattern_key: bfloat16 [2048, 1536], P('grp'), may hold values from -4.5 to 4.5
- pattern_value: bfloat16 [2048, 1536], P('grp'), may hold values from -6 to 6
- pencil_order: int32 [128], replicated, may hold values from 0 to 127, as said below
Outputs:
- query_grad: bfloat16 [2048, 1536], P(('blk', 'grp'))
- key_grad: bfloat16 [2048, 1536], P(('blk', 'grp'))
- value_grad: bfloat16 [2048, 1536], P(('blk', 'grp'))
Inputs may be any that keep to these rules, and one draw needn't show every extreme that they name: pencil_order is a permutation of 0 to 127. With c the number of devices along grp, block r of the encoder's layout lies on the device of index r // 4 of the axes blk+grp, and pencil_order[r] names a block of pattern rows g * 256 to (g + 1) * 256 - 1, where g is that device index mod c.
All inputs are finite; a program needn't handle non-finite values.
Results may differ from a plain program's by a relative error of at most 0.0051.
Values may be sent and summed in bfloat16 or wider, within the bound.
A program may use at most 128 MiB of HBM per device.

v0:
```python
import math

import jax
import jax.numpy as jnp
from jax import lax
from jax.sharding import PartitionSpec as P

H = 16
PENCIL = 16


def joined(value, axis, combine):
    everything = jax.tree.map(lambda part: lax.all_gather(part, axis), value)
    initial = jax.tree.map(lambda part: part[0], everything)

    def step(k, so_far):
        return combine(so_far, jax.tree.map(lambda part: part[k], everything))

    return lax.fori_loop(1, lax.axis_size(axis), step, initial)


def split_heads(matrix):
    return matrix.reshape(matrix.shape[0], H, matrix.shape[1] // H)


def block_stats(part_query, part_grad, key_block, value_block):
    scaling = 1.0 / math.sqrt(key_block.shape[1] // H)
    scores = (
        jnp.einsum(
            "rhd,chd->hrc",
            split_heads(part_query),
            split_heads(key_block),
            preferred_element_type=jnp.float32,
        )
        * scaling
    )
    prob_grad = jnp.einsum(
        "rhd,chd->hrc",
        split_heads(part_grad),
        split_heads(value_block),
        preferred_element_type=jnp.float32,
    )
    highest = jnp.max(scores, axis=2)
    weights = jnp.exp(scores - highest[:, :, None])
    return (highest, jnp.sum(weights, axis=2), jnp.sum(weights * prob_grad, axis=2))


def join_stats(earlier, later):
    highest = jnp.maximum(earlier[0], later[0])
    before = jnp.exp(earlier[0] - highest)
    after = jnp.exp(later[0] - highest)
    return (highest, earlier[1] * before + later[1] * after, earlier[2] * before + later[2] * after)


def stats_of_rows(queries, grads, key_block, value_block):
    amount, features = queries.shape
    blocking = math.gcd(amount, 128)

    def one_block(couple):
        return block_stats(couple[0], couple[1], key_block, value_block)

    stacked = lax.map(
        one_block,
        (
            queries.reshape(amount // blocking, blocking, features),
            grads.reshape(amount // blocking, blocking, features),
        ),
    )
    return tuple((jnp.moveaxis(member, 0, 1).reshape(H, amount) for member in stacked))


def block_grads(part_query, part_grad, log_now, mean_now, key_block, value_block):
    features = key_block.shape[1]
    scaling = 1.0 / math.sqrt(features // H)
    query_heads = split_heads(part_query)
    grad_heads = split_heads(part_grad)
    key_heads = split_heads(key_block)
    value_heads = split_heads(value_block)
    scores = (
        jnp.einsum("rhd,chd->hrc", query_heads, key_heads, preferred_element_type=jnp.float32)
        * scaling
    )
    prob_grad = jnp.einsum(
        "rhd,chd->hrc", grad_heads, value_heads, preferred_element_type=jnp.float32
    )
    softmax = jnp.exp(scores - log_now[:, :, None])
    softmax_low = softmax.astype(jnp.bfloat16)
    score_grad = (scaling * softmax * (prob_grad - mean_now[:, :, None])).astype(jnp.bfloat16)
    query_term = jnp.einsum(
        "hrc,chd->rhd", score_grad, key_heads, preferred_element_type=jnp.float32
    ).reshape(part_query.shape[0], features)
    key_term = jnp.einsum(
        "hrc,rhd->chd", score_grad, query_heads, preferred_element_type=jnp.float32
    ).reshape(key_block.shape[0], features)
    value_term = jnp.einsum(
        "hrc,rhd->chd", softmax_low, grad_heads, preferred_element_type=jnp.float32
    ).reshape(key_block.shape[0], features)
    return (query_term, key_term, value_term)


def on_device(obj_query, grad_out, pattern_key, pattern_value, pencil_order):
    amount, features = obj_query.shape
    columns = pattern_key.shape[0]
    groups = lax.axis_size("grp")
    position = lax.axis_index("grp")
    group_rows = groups * amount
    all_query, all_grad = (
        lax.all_gather(obj_query, "grp", axis=0, tiled=True),
        lax.all_gather(grad_out, "grp", axis=0, tiled=True),
    )
    partial_value = stats_of_rows(all_query, all_grad, pattern_key, pattern_value)
    highest, totals, weighted = joined(partial_value, "grp", join_stats)
    log_totals = highest + jnp.log(totals)
    mean_grads = weighted / totals
    blocking = math.gcd(group_rows, 128)
    sweeps = group_rows // blocking

    def sweep(carried, segment):
        keys_acc, values_acc = carried
        query_term, key_term, value_term = block_grads(
            segment[0], segment[1], segment[2], segment[3], pattern_key, pattern_value
        )
        return ((keys_acc + key_term, values_acc + value_term), query_term)

    log_blocks = jnp.moveaxis(log_totals.reshape(H, sweeps, blocking), 1, 0)
    mean_blocks = jnp.moveaxis(mean_grads.reshape(H, sweeps, blocking), 1, 0)
    zeros_acc = jnp.zeros((columns, features), jnp.float32)
    segments = (
        all_query.reshape(sweeps, blocking, features),
        all_grad.reshape(sweeps, blocking, features),
        log_blocks,
        mean_blocks,
    )
    (keys_acc, values_acc), pieces = lax.scan(sweep, (zeros_acc, zeros_acc), segments)
    query_total = lax.psum_scatter(
        pieces.reshape(group_rows, features), "grp", scatter_dimension=0, tiled=True
    )
    device_rows = columns // lax.axis_size("blk")
    spots = jnp.arange(columns, dtype=jnp.int32)
    target = (spots // device_rows * groups + position) * device_rows + spots % device_rows
    source = (
        jnp.take(pencil_order, target // PENCIL) * PENCIL + target % PENCIL - position * columns
    )
    combined = lax.psum_scatter(
        jnp.concatenate(
            [jnp.take(keys_acc, source, axis=0), jnp.take(values_acc, source, axis=0)], axis=1
        ),
        "blk",
        scatter_dimension=0,
        tiled=True,
    )
    key_grad = combined[:, :features].astype(jnp.bfloat16)
    value_grad = combined[:, features:].astype(jnp.bfloat16)
    return (query_total.astype(jnp.bfloat16), key_grad, value_grad)


def solution(mesh):
    in_specs = (
        P(("blk", "grp"), None),
        P(("blk", "grp"), None),
        P("grp", None),
        P("grp", None),
        P(),
    )
    out_specs = (P(("blk", "grp"), None), P(("blk", "grp"), None), P(("blk", "grp"), None))
    return jax.shard_map(
        on_device, mesh=mesh, in_specs=in_specs, out_specs=out_specs, check_vma=False
    )
```

profile of v0, /device:TPU:0, one launch (start us, length us, event | category | flops | bytes accessed | tf_op | source)
XLA Modules:
  0.0 297.5 jit_solution(10365275164797031814)
XLA Ops:
  8.8 1.4 copy.42
  10.5 27.9 %all-gather.3.cloned.1.call-done = bf16[512,1536]{1,0:T(8,128)(2,1)} async-done(((bf16[64,1536]{1,0:T(8,128)(2,1)}), bf16[512,1536]{1,0:T(8,128)(2,1)}) %all-gather.3.cloned.1.call-update) | async-done | bytes 1572880 | tf_op jit(solution)/shard_map/all_gather | solution.py:108
  38.3 2.6 copy.41
  40.9 25.0 %all-gather.5.cloned.1.call-done = bf16[512,1536]{1,0:T(8,128)(2,1)} async-done(((bf16[64,1536]{1,0:T(8,128)(2,1)}), bf16[512,1536]{1,0:T(8,128)(2,1)}) %all-gather.5.cloned.1.call-update) | async-done | bytes 1572880 | tf_op jit(solution)/shard_map/all_gather | solution.py:109
  65.9 2.6 copy.36
  68.5 17.7 %while.48 = (s32[]{:T(128)}, f32[4,16,128]{2,1,0:T(8,128)S(1)}, f32[4,16,128]{2,1,0:T(8,128)S(1)}, f32[4,16,128]{2,1,0:T(8,128)S(1)}, bf16[4,128,1536]{1,2,0:T(8...) while((s32[]{:T(128)}, f32[4,16,128]{2,1,0:T(8,128)S(1)}, ...), condition=%wide.region_4.5_spmd, body=%wide.region_0.4_spmd.sunk | while | flops 206039040 | bytes 10313845 | solution.py:62
  68.5 1.0 constant_dynamic-slice_fusion.13
  69.6 1.0 constant_dynamic-slice_fusion.12
  71.2 1.0 multiply_reduce_fusion.5
  73.0 1.0 constant_dynamic-slice_fusion.13
  74.0 1.0 constant_dynamic-slice_fusion.12
  75.6 1.0 multiply_reduce_fusion.5
  77.4 1.0 constant_dynamic-slice_fusion.13
  78.4 1.0 constant_dynamic-slice_fusion.12
  80.0 1.0 multiply_reduce_fusion.5
  81.8 1.0 constant_dynamic-slice_fusion.13
  82.9 1.0 constant_dynamic-slice_fusion.12
  84.5 1.0 multiply_reduce_fusion.5
  86.4 9.3 %all_gather.18 = f32[8,16,512]{2,1,0:T(8,128)S(1)} all-gather(f32[1,16,512]{2,1,0:T(8,128)S(1)} %all_gather_reshape.10), channel_id=1, replica_groups=mesh['blk'=4,'grp'=8] {'grp'}, dimensions={0}, use_global_device_ids=true | all-gather | bytes 294912 | tf_op jit(solution)/shard_map/all_gather | solution.py:13
  95.7 8.3 %all_gather.17 = f32[8,16,512]{2,1,0:T(8,128)S(1)} all-gather(f32[1,16,512]{2,1,0:T(8,128)S(1)} %all_gather_reshape.9), channel_id=1, replica_groups=mesh['blk'=4,'grp'=8] {'grp'}, dimensions={0}, use_global_device_ids=true | all-gather | bytes 294912 | tf_op jit(solution)/shard_map/all_gather | solution.py:13
  104.0 9.3 %all_gather.19 = f32[8,16,512]{2,1,0:T(8,128)S(1)} all-gather(f32[1,16,512]{2,1,0:T(8,128)S(1)} %all_gather_reshape.11), channel_id=1, replica_groups=mesh['blk'=4,'grp'=8] {'grp'}, dimensions={0}, use_global_device_ids=true | all-gather | bytes 294912 | tf_op jit(solution)/shard_map/all_gather | solution.py:13
  114.1 66.0 %while.50 = (s32[]{:T(128)}, f32[256,1536]{0,1:T(8,128)}, f32[256,1536]{0,1:T(8,128)}, f32[4,128,1536]{2,1,0:T(8,128)}, bf16[4,128,1536]{1,2,0:T(8,128)(2,1)}, /...) while((s32[]{:T(128)}, f32[256,1536]{0,1:T(8,128)}, ...), condition=%wide.region_8.9_spmd.clone, body=%wide.region_7.8_spmd.clone.sunk | while | flops 509607936 | bytes 53535012 | solution.py:134
  114.1 1.3 constant_dynamic-slice_fusion.14
  115.4 1.8 constant_dynamic-slice_fusion.15
  117.2 1.5 fusion.78
  118.7 1.1 multiply_convert_fusion.2
  120.6 1.3 fusion.81
  122.0 2.3 copy.55
  124.2 1.5 fusion.80
  125.8 2.1 bitcast_add_fusion.3
  129.6 1.3 constant_dynamic-slice_fusion.14
  130.8 1.8 constant_dynamic-slice_fusion.15
  132.6 1.5 fusion.78
  134.1 1.1 multiply_convert_fusion.2
  136.1 1.3 fusion.81
  137.4 2.3 copy.55
  139.7 1.5 fusion.80
  141.2 3.5 %bitcast_add_fusion.3 = (f32[256,1536]{0,1:T(8,128)S(1)}, f32[256,1536]{0,1:T(8,128)}) fusion(f32[16,96,256]{2,1,0:T(8,128)S(1)} %fusion.79, f32[256,1536]{0,1:T(8,128)S(1)} %copy-done.4, pred[]{:T(512)S(6)} %compare.28, f32[16,96,256]{2,1,0:T(8,128)S(1)} %fusion.80, f32[256,1536]{0,1:T(8,128)} %get-tuple-element.681), kind=kLoop, calls=%fused_computation.23.clone.1 | loop fusion | flops 1572864 | bytes 9437185 | tf_op jit(solution)/shard_map/while/body/eval_jaxpr/add | solution.py:123
  146.4 1.3 constant_dynamic-slice_fusion.14
  147.7 1.8 constant_dynamic-slice_fusion.15
  149.4 1.5 fusion.78
  150.9 1.1 multiply_convert_fusion.2
  152.9 1.3 fusion.81
  154.2 2.3 copy.55
  156.5 1.5 fusion.80
  158.1 3.5 %bitcast_add_fusion.3 = (f32[256,1536]{0,1:T(8,128)S(1)}, f32[256,1536]{0,1:T(8,128)}) fusion(f32[16,96,256]{2,1,0:T(8,128)S(1)} %fusion.79, f32[256,1536]{0,1:T(8,128)S(1)} %copy-done.4, pred[]{:T(512)S(6)} %compare.28, f32[16,96,256]{2,1,0:T(8,128)S(1)} %fusion.80, f32[256,1536]{0,1:T(8,128)} %get-tuple-element.681), kind=kLoop, calls=%fused_computation.23.clone.1 | loop fusion | flops 1572864 | bytes 9437185 | tf_op jit(solution)/shard_map/while/body/eval_jaxpr/add | solution.py:123
  163.2 1.3 constant_dynamic-slice_fusion.14
  164.5 1.8 constant_dynamic-slice_fusion.15
  166.3 1.5 fusion.78
  167.8 1.1 multiply_convert_fusion.2
  169.8 1.3 fusion.81
  171.1 2.3 copy.55
  173.4 1.5 fusion.80
  174.9 3.5 %bitcast_add_fusion.3 = (f32[256,1536]{0,1:T(8,128)S(1)}, f32[256,1536]{0,1:T(8,128)}) fusion(f32[16,96,256]{2,1,0:T(8,128)S(1)} %fusion.79, f32[256,1536]{0,1:T(8,128)S(1)} %copy-done.4, pred[]{:T(512)S(6)} %compare.28, f32[16,96,256]{2,1,0:T(8,128)S(1)} %fusion.80, f32[256,1536]{0,1:T(8,128)} %get-tuple-element.681), kind=kLoop, calls=%fused_computation.23.clone.1 | loop fusion | flops 1572864 | bytes 9437185 | tf_op jit(solution)/shard_map/while/body/eval_jaxpr/add | solution.py:123
  180.4 1.9 gather_fusion
  182.8 1.9 copy.49
  184.6 2.3 gather_fusion.1
  187.0 2.4 gather_fusion.2
  189.4 2.0 broadcast_select_fusion.1
  191.3 1.9 pad_maximum_fusion
  193.3 33.2 %reduce-scatter.3.cloned.1.call-done = f32[64,1536]{1,0:T(8,128)} async-done(((f32[512,1536]{1,0:T(8,128)}), f32[64,1536]{1,0:T(8,128)}) %reduce-scatter.3.cloned.1.call-update) | async-done | bytes 393232 | tf_op jit(solution)/shard_map/reduce_scatter | solution.py:135
  226.5 1.7 convert_element_type.11
  228.2 60.9 %reduce-scatter.5.cloned.1.call-done = f32[64,3072]{1,0:T(8,128)} async-done(((f32[256,3072]{1,0:T(8,128)}), f32[64,3072]{1,0:T(8,128)}) %reduce-scatter.5.cloned.1.call-update) | async-done | bytes 786448 | tf_op jit(solution)/shard_map/reduce_scatter | solution.py:144
  289.0 1.2 convert.4
  (135 shorter events, 20.5 us)
Async XLA Ops:
  7.2 173.2 %copy-start = (s32[128]{0:T(128)S(1)}, s32[128]{0:T(128)}, u32[]{:S(2)}) copy-start(s32[128]{0:T(128)} %param.17) | copy-start | bytes 1540
  7.2 3.0 %copy-start.8 = (bf16[256,1536]{1,0:T(8,128)(2,1)S(1)}, bf16[256,1536]{1,0:T(8,128)(2,1)}, u32[]{:S(2)}) copy-start(bf16[256,1536]{1,0:T(8,128)(2,1)} %param.16) | copy-start | bytes 2359300
  7.2 31.1 %all-gather.3.cloned.1.call-start = ((), (), s32[]{:S(2)}) async-start(), calls=%async_computation.2 | async-start | bytes 1769472 | tf_op jit(solution)/shard_map/all_gather | solution.py:108
  7.9 58.0 %all-gather.5.cloned.1.call-start = ((), (), s32[]{:S(2)}) async-start(), calls=%async_computation.3 | async-start | bytes 1769472 | tf_op jit(solution)/shard_map/all_gather | solution.py:109
  8.7 217.8 %reduce-scatter.3.cloned.1.call-start = ((), (), s32[]{:S(2)}) async-start(), calls=%async_computation.4 | async-start | bytes 3538944 | tf_op jit(solution)/shard_map/reduce_scatter | solution.py:135
  114.1 4.6 %copy-start.1 = (bf16[256,1536]{0,1:T(8,128)(2,1)}, bf16[256,1536]{0,1:T(8,128)(2,1)S(1)}, u32[]{:S(2)}) copy-start(bf16[256,1536]{0,1:T(8,128)(2,1)S(1)} %get-tuple-element.700) | copy-start | bytes 2359300 | tf_op jit(solution)/shard_map/while
  124.2 1.5 copy-start.4
  125.8 2.1 copy-start.3
  127.8 1.5 copy-start.5
  127.8 1.7 copy-start.2
  129.5 4.6 %copy-start.1 = (bf16[256,1536]{0,1:T(8,128)(2,1)}, bf16[256,1536]{0,1:T(8,128)(2,1)S(1)}, u32[]{:S(2)}) copy-start(bf16[256,1536]{0,1:T(8,128)(2,1)S(1)} %get-tuple-element.700) | copy-start | bytes 2359300 | tf_op jit(solution)/shard_map/while
  139.7 1.5 copy-start.4
  141.2 3.5 %copy-start.3 = (f32[1,128,1536]{2,1,0:T(8,128)S(1)}, f32[1,128,1536]{2,1,0:T(8,128)}, u32[]{:S(2)}) copy-start(f32[1,128,1536]{2,1,0:T(8,128)} %copy.55) | copy-start | bytes 2359300 | tf_op jit(solution)/shard_map/while
  144.7 1.5 copy-start.5
  144.7 1.7 copy-start.2
  146.4 4.6 %copy-start.1 = (bf16[256,1536]{0,1:T(8,128)(2,1)}, bf16[256,1536]{0,1:T(8,128)(2,1)S(1)}, u32[]{:S(2)}) copy-start(bf16[256,1536]{0,1:T(8,128)(2,1)S(1)} %get-tuple-element.700) | copy-start | bytes 2359300 | tf_op jit(solution)/shard_map/while
  156.5 1.5 copy-start.4
  158.1 3.5 %copy-start.3 = (f32[1,128,1536]{2,1,0:T(8,128)S(1)}, f32[1,128,1536]{2,1,0:T(8,128)}, u32[]{:S(2)}) copy-start(f32[1,128,1536]{2,1,0:T(8,128)} %copy.55) | copy-start | bytes 2359300 | tf_op jit(solution)/shard_map/while
  161.5 1.5 copy-start.5
  161.5 1.7 copy-start.2
  163.2 4.6 %copy-start.1 = (bf16[256,1536]{0,1:T(8,128)(2,1)}, bf16[256,1536]{0,1:T(8,128)(2,1)S(1)}, u32[]{:S(2)}) copy-start(bf16[256,1536]{0,1:T(8,128)(2,1)S(1)} %get-tuple-element.700) | copy-start | bytes 2359300 | tf_op jit(solution)/shard_map/while
  173.4 1.5 copy-start.4
  174.9 3.5 %copy-start.3 = (f32[1,128,1536]{2,1,0:T(8,128)S(1)}, f32[1,128,1536]{2,1,0:T(8,128)}, u32[]{:S(2)}) copy-start(f32[1,128,1536]{2,1,0:T(8,128)} %copy.55) | copy-start | bytes 2359300 | tf_op jit(solution)/shard_map/while
  178.4 1.5 copy-start.5
  178.4 1.7 copy-start.2
  180.0 2.2 copy-start.6
  180.1 109.0 %reduce-scatter.5.cloned.1.call-start = ((), (), s32[]{:S(2)}) async-start(), calls=%async_computation.5 | async-start | bytes 3932160 | tf_op jit(solution)/shard_map/reduce_scatter | solution.py:144
  187.0 2.4 copy-start.7
Sparse Core Ops, SparseCore 0:
  9.9 28.3 all-gather.2
  40.2 25.6 all-gather.4
  180.2 46.2 reduce-scatter.2
  228.7 60.2 reduce-scatter.4
where the time goes:
time: 299 us; the launch traced here: 298 us
  waiting for transfers between devices  148 us (49%)
  local copies, waits for them, and re-layouts  53.3 us (18%)
  matrix products  31.2 us (10%)
  blocking collectives  26.9 us (9%)
  other arithmetic  22.8 us (8%)
  between operations  14 us (5%)
    reduce_scatter x1, waiting for transfers between devices, on_device(): lax.psum_scatter(jnp.concatenate([jnp.take(keys_acc, source, axis=0), jnp...  60.9 us
    reduce_scatter x1, waiting for transfers between devices, on_device(): lax.psum_scatter(pieces.reshape(group_rows, features), 'grp', scatter_dim...  33.2 us
    all_gather x1, waiting for transfers between devices, on_device(): lax.all_gather(obj_query, 'grp', axis=0, tiled=True)  27.9 us
    all_gather x3, blocking collectives, joined(): everything = jax.tree.map(lambda part: lax.all_gather(part, axis), value)  26.9 us
    all_gather x1, waiting for transfers between devices, on_device(): lax.all_gather(grad_out, 'grp', axis=0, tiled=True)  25 us
    dynamic_slice x16, local copies, waits for them, and re-layouts, stats_of_rows(): lax.map(one_block, (queries.reshape(amount // blocking, blocking, feature...  20.4 us
    dynamic_update_slice x8, local copies, waits for them, and re-layouts, on_device(): lax.scan(sweep, (zeros_acc, zeros_acc), segments)  12.9 us
    add x4, other arithmetic, sweep(): return ((keys_acc + key_term, values_acc + value_term), query_term)  12.4 us
  transfers between devices with their start and end apart: 4, of which 4 were waited for; matrix products, arithmetic and copies ran while one was open for 6% of the time, Pallas kernels for 0%

commit v1 on v0

--- a/solution.py
+++ b/solution.py
@@ -1,8 +1,11 @@
+import functools
 import math
 
 import jax
 import jax.numpy as jnp
 from jax import lax
+from jax.experimental import pallas as pl
+from jax.experimental.pallas import tpu as pltpu
 from jax.sharding import PartitionSpec as P
 
 H = 16
@@ -154,6 +157,333 @@
     return (query_total.astype(jnp.bfloat16), key_grad, value_grad)
 
 
+MESH = pl.DeviceIdType.MESH
+F32 = jnp.float32
+BF16 = jnp.bfloat16
+
+
+def mm(a, b, ca, cb):
+    return lax.dot_general(a, b, (((ca,), (cb,)), ((), ())), preferred_element_type=F32)
+
+
+def turn(x):
+    return x.T
+
+
+def fused(
+    n_blk,
+    n_grp,
+    hd,
+    q_ref,
+    g_ref,
+    k_ref,
+    v_ref,
+    order_ref,
+    oq_ref,
+    ok_ref,
+    ov_ref,
+    kvt_own,
+    kvt,
+    qz,
+    qgt_own,
+    qgt,
+    s_buf,
+    d_buf,
+    kvacc,
+    kvsend,
+    rkv,
+    pst,
+    full_kv,
+    qg,
+    qst,
+    full_q,
+    onehot,
+    zst,
+    kv_ss,
+    kv_rs,
+    z_ss,
+    z_rs,
+    pq_ss,
+    pq_rs,
+    r_ss,
+    r_rs,
+    pk_ss,
+    pk_rs,
+    po_ss,
+    po_rs,
+    o_ss,
+    o_rs,
+):
+    b = lax.axis_index("blk")
+    g = lax.axis_index("grp")
+    chips = n_grp // 2
+    p = g // 2
+    c = g % 2
+    partner = 2 * p + 1 - c
+    rows = q_ref.shape[0]
+    cols = k_ref.shape[0]
+    nk = cols * n_grp
+    gw = 4 * hd
+    scaling = 1.0 / math.sqrt(hd)
+    expc = scaling * math.log2(math.e)
+
+    def lanes(index, width):
+        return pl.ds(pl.multiple_of(index * width, width), width)
+
+    def remote(src, dst, ss, rs, bb, gg):
+        copy = pltpu.make_async_remote_copy(
+            src_ref=src,
+            dst_ref=dst,
+            send_sem=ss,
+            recv_sem=rs,
+            device_id=(bb, gg),
+            device_id_type=MESH,
+        )
+        copy.start()
+        return copy
+
+    barrier = pltpu.get_barrier_semaphore()
+    for d in range(1, n_grp):
+        pl.semaphore_signal(barrier, inc=1, device_id=(b, (g + d) % n_grp), device_id_type=MESH)
+    for d in range(1, n_blk):
+        pl.semaphore_signal(barrier, inc=1, device_id=((b + d) % n_blk, g), device_id_type=MESH)
+
+    for t, ref in enumerate((k_ref, v_ref)):
+        part = turn(ref[:, lanes(b, gw)])
+        for hl in range(4):
+            kvt_own[hl, t] = part[hd * hl : hd * hl + hd]
+    pl.semaphore_wait(barrier, n_grp + n_blk - 2)
+
+    z_copies = []
+    for d in range(1, n_blk):
+        bb = (b + d) % n_blk
+        for t, ref in enumerate((q_ref, g_ref)):
+            z_copies.append(
+                remote(
+                    ref.at[:, lanes(bb, gw)],
+                    qz.at[t, lanes(b, rows), :],
+                    z_ss.at[d - 1, t],
+                    z_rs.at[d - 1, t],
+                    bb,
+                    g,
+                )
+            )
+    kv_copies = {}
+    for h in range(2):
+        for d in range(1, n_grp):
+            gg = (g + d) % n_grp
+            kv_copies[h, d] = remote(
+                kvt_own.at[2 * (gg % 2) + h],
+                kvt.at[h, :, :, lanes(g, cols)],
+                kv_ss.at[d - 1, h],
+                kv_rs.at[d - 1, h],
+                b,
+                gg,
+            )
+    for h in range(2):
+        for t in range(2):
+            kvt[h, t, :, lanes(g, cols)] = kvt_own[2 * c + h, t]
+    for t, ref in enumerate((q_ref, g_ref)):
+        qz[t, lanes(b, rows), :] = ref[:, lanes(b, gw)]
+
+    row = lax.broadcasted_iota(jnp.int32, (PENCIL, cols), 0)
+    col = lax.broadcasted_iota(jnp.int32, (PENCIL, cols), 1)
+    per = rows // PENCIL
+    for bb in range(n_blk):
+        for k in range(per):
+            first = order_ref[(bb * n_grp + g) * per + k] * PENCIL - g * cols
+            onehot[pl.ds(bb * rows + k * PENCIL, PENCIL), :] = jnp.where(
+                col - row == first, 1.0, 0.0
+            ).astype(BF16)
+
+    for copy in z_copies:
+        copy.wait_recv()
+    for t in range(2):
+        part = turn(qz[t])
+        for hl in range(4):
+            qgt_own[hl, t] = part[hd * hl : hd * hl + hd]
+    pair_q = remote(
+        qgt_own.at[pl.ds(2 * (1 - c), 2)],
+        qgt.at[:, :, :, lanes(c, cols)],
+        pq_ss,
+        pq_rs,
+        b,
+        partner,
+    )
+    for h in range(2):
+        for t in range(2):
+            qgt[h, t, :, lanes(c, cols)] = qgt_own[2 * c + h, t]
+    pair_q.wait_recv()
+
+    r_copies = {}
+    wide = 256
+    for h in range(2):
+        for d in range(1, n_grp):
+            kv_copies[h, d].wait_recv()
+        kvacc[h] = jnp.zeros_like(kvacc[h])
+
+        def block(j, carry):
+            qt = qgt[h, 0, :, lanes(j, cols)]
+            gt = qgt[h, 1, :, lanes(j, cols)]
+            qb = turn(qt)
+            gb = turn(gt)
+            top = jnp.full((cols, wide), -jnp.inf, F32)
+            for n in range(nk // wide):
+                at = pl.ds(n * wide, wide)
+                s = mm(qb, kvt[h, 0, :, at], 1, 0)
+                s_buf[:, at] = s
+                top = jnp.maximum(top, s)
+            top = jnp.max(top, axis=1, keepdims=True)
+            tot = jnp.zeros((cols, wide), F32)
+            wtd = jnp.zeros((cols, wide), F32)
+            for n in range(nk // wide):
+                at = pl.ds(n * wide, wide)
+                e = jnp.exp2((s_buf[:, at] - top) * expc)
+                dp = mm(gb, kvt[h, 1, :, at], 1, 0)
+                s_buf[:, at] = e
+                d_buf[:, at] = dp
+                tot = tot + e
+                wtd = wtd + e * dp
+            inv = 1.0 / jnp.sum(tot, axis=1, keepdims=True)
+            mean = jnp.sum(wtd, axis=1, keepdims=True) * inv
+            acc = jnp.zeros((cols, hd), F32)
+            for n in range(nk // wide):
+                at = pl.ds(n * wide, wide)
+                soft = s_buf[:, at] * inv
+                low = soft.astype(BF16)
+                sg = (scaling * soft * (d_buf[:, at] - mean)).astype(BF16)
+                kvacc[h, 0, :, at] += mm(qt, sg, 1, 0)
+                kvacc[h, 1, :, at] += mm(gt, low, 1, 0)
+                acc = acc + mm(sg, kvt[h, 0, :, at], 1, 1)
+            qg[h, lanes(j, cols), :] = acc
+            return carry
+
+        lax.fori_loop(0, 2, block, 0)
+        kvsend[h] = kvacc[h].astype(BF16)
+        for e in range(1, chips):
+            pp = (p + e) % chips
+            r_copies[h, e] = remote(
+                kvsend.at[h, :, :, lanes(pp, 2 * cols)],
+                rkv.at[e - 1, h],
+                r_ss.at[e - 1, h],
+                r_rs.at[e - 1, h],
+                b,
+                2 * pp + c,
+            )
+
+    for h in range(2):
+        qst[h] = turn(qg[h, lanes(1 - c, cols), :]).astype(BF16)
+    pair_o = remote(qst, full_q.at[pl.ds(2 * c, 2)], po_ss, po_rs, b, partner)
+    for h in range(2):
+        full_q[2 * c + h] = turn(qg[h, lanes(c, cols), :]).astype(BF16)
+    pair_o.wait_recv()
+
+    out_copies = []
+
+    def deliver(t, value, out):
+        zst[t] = value
+        for d in range(1, n_blk):
+            bb = (b + d) % n_blk
+            out_copies.append(
+                remote(
+                    zst.at[t, lanes(bb, rows), :],
+                    out.at[:, lanes(b, gw)],
+                    o_ss.at[d - 1, t],
+                    o_rs.at[d - 1, t],
+                    bb,
+                    g,
+                )
+            )
+        out[:, lanes(b, gw)] = zst[t, lanes(b, rows), :]
+
+    deliver(0, turn(full_q[...].reshape(gw, cols)), oq_ref)
+
+    pair_k = []
+    for h in range(2):
+        for e in range(1, chips):
+            r_copies[h, e].wait_recv()
+
+        def summed(part):
+            at = pl.ds(pl.multiple_of(p * 2 * cols + part * cols, cols), cols)
+            total = kvacc[h, :, :, at]
+            for e in range(1, chips):
+                total = total + rkv[e - 1, h, :, :, lanes(part, cols)].astype(F32)
+            return total.astype(BF16)
+
+        pst[h] = summed(1 - c)
+        pair_k.append(
+            remote(pst.at[h], full_kv.at[2 * c + h], pk_ss.at[h], pk_rs.at[h], b, partner)
+        )
+        full_kv[2 * c + h] = summed(c)
+    for copy in pair_k:
+        copy.wait_recv()
+    for t, out in enumerate((ok_ref, ov_ref)):
+        both = full_kv[:, t].reshape(gw, cols)
+        deliver(1 + t, mm(onehot[...], both, 1, 1).astype(BF16), out)
+
+    for copy in out_copies:
+        copy.wait_recv()
+    for copy in [*z_copies, *kv_copies.values(), *r_copies.values(), *pair_k, *out_copies]:
+        copy.wait_send()
+    pair_q.wait_send()
+    pair_o.wait_send()
+
+
+def fused_on_device(n_blk, n_grp, obj_query, grad_out, pattern_key, pattern_value, pencil_order):
+    rows, features = obj_query.shape
+    cols = pattern_key.shape[0]
+    hd = features // H
+    nk = cols * n_grp
+    chips = n_grp // 2
+    gw = 4 * hd
+    dma = pltpu.SemaphoreType.DMA
+    vmem = pl.BlockSpec(memory_space=pltpu.VMEM)
+    return tuple(
+        pl.pallas_call(
+            functools.partial(fused, n_blk, n_grp, hd),
+            out_shape=[jax.ShapeDtypeStruct((rows, features), BF16)] * 3,
+            in_specs=[vmem] * 4 + [pl.BlockSpec(memory_space=pltpu.SMEM)],
+            out_specs=[vmem] * 3,
+            scratch_shapes=[
+                pltpu.VMEM((4, 2, hd, cols), BF16),
+                pltpu.VMEM((2, 2, hd, nk), BF16),
+                pltpu.VMEM((2, cols, gw), BF16),
+                pltpu.VMEM((4, 2, hd, cols), BF16),
+                pltpu.VMEM((2, 2, hd, 2 * cols), BF16),
+                pltpu.VMEM((cols, nk), F32),
+                pltpu.VMEM((cols, nk), F32),
+                pltpu.VMEM((2, 2, hd, nk), F32),
+                pltpu.VMEM((2, 2, hd, nk), BF16),
+                pltpu.VMEM((chips - 1, 2, 2, hd, 2 * cols), BF16),
+                pltpu.VMEM((2, 2, hd, cols), BF16),
+                pltpu.VMEM((4, 2, hd, cols), BF16),
+                pltpu.VMEM((2, 2 * cols, hd), F32),
+                pltpu.VMEM((2, hd, cols), BF16),
+                pltpu.VMEM((4, hd, cols), BF16),
+                pltpu.VMEM((cols, cols), BF16),
+                pltpu.VMEM((3, cols, gw), BF16),
+                dma((n_grp - 1, 2)),
+                dma((n_grp - 1, 2)),
+                dma((n_blk - 1, 2)),
+                dma((n_blk - 1, 2)),
+                dma,
+                dma,
+                dma((chips - 1, 2)),
+                dma((chips - 1, 2)),
+                dma((2,)),
+                dma((2,)),
+                dma,
+                dma,
+                dma((n_blk - 1, 3)),
+                dma((n_blk - 1, 3)),
+            ],
+            compiler_params=pltpu.CompilerParams(
+                collective_id=0, has_side_effects=True, vmem_limit_bytes=48 * 1024 * 1024
+            ),
+        )(obj_query, grad_out, pattern_key, pattern_value, pencil_order)
+    )
+
+
 def solution(mesh):
     in_specs = (
         P(("blk", "grp"), None),
@@ -163,6 +493,17 @@
         P(),
     )
     out_specs = (P(("blk", "grp"), None), P(("blk", "grp"), None), P(("blk", "grp"), None))
-    return jax.shard_map(
-        on_device, mesh=mesh, in_specs=in_specs, out_specs=out_specs, check_vma=False
-    )
+    n_blk, n_grp = mesh.shape["blk"], mesh.shape["grp"]
+
+    def body(obj_query, grad_out, pattern_key, pattern_value, pencil_order):
+        features = obj_query.shape[1]
+        fits = (
+            n_blk * 4 == H
+            and (features // n_blk) % 128 == 0
+            and pattern_key.shape[0] == 256
+            and n_blk * obj_query.shape[0] == 256
+        )
+        step = functools.partial(fused_on_device, n_blk, n_grp) if fits else on_device
+        return step(obj_query, grad_out, pattern_key, pattern_value, pencil_order)
+
+    return jax.shard_map(body, mesh=mesh, in_specs=in_specs, out_specs=out_specs, check_vma=False)

time: 299 us -> 60.2 us (0.20)
  waiting for transfers between devices: 148 us -> 0 us
  Pallas kernels: 0 us -> 52.5 us
  local copies, waits for them, and re-layouts: 53.3 us -> 6.8 us
  matrix products: 31.2 us -> 0 us
  blocking collectives: 26.9 us -> 0 us
  other arithmetic: 22.8 us -> 0 us
  between operations: 14 us -> 0.65 us
    reduce_scatter x2 -> x0, waiting for transfers between devices: 94 us -> none  [the longest x1 60.9 us: on_device(): lax.psum_scatter(jnp.concatenate([jnp.take(keys_acc, source, axis=0), jnp...]
    all_gather x2 -> x0, waiting for transfers between devices: 52.9 us -> none  [the longest x1 27.9 us: on_device(): lax.all_gather(obj_query, 'grp', axis=0, tiled=True)]
    pallas_call x0 -> x1, Pallas kernels: none -> 52.5 us  [fused_on_device(): pl.pallas_call(functools.partial(fused, n_blk, n_grp, hd), out_shape=[jax...]
    dot_general x28 -> x0, matrix products: 31.2 us -> none  [the longest x4 5.92 us: block_grads(): jnp.einsum('hrc,rhd->chd', score_grad, query_heads, preferred_element_typ...]
    all_gather x3 -> x0, blocking collectives: 26.9 us -> none  [joined(): everything = jax.tree.map(lambda part: lax.all_gather(part, axis), value)]
    dynamic_slice x24 -> x0, local copies, waits for them, and re-layouts: 20.5 us -> none  [the longest x16 20.4 us: stats_of_rows(): lax.map(one_block, (queries.reshape(amount // blocking, blocking, feature...]
    dynamic_update_slice x16 -> x0, local copies, waits for them, and re-layouts: 13 us -> none  [the longest x8 12.9 us: on_device(): lax.scan(sweep, (zeros_acc, zeros_acc), segments)]
    add x18 -> x0, other arithmetic: 12.9 us -> none  [the longest x4 12.4 us: sweep(): return ((keys_acc + key_term, values_acc + value_term), query_term)]
  transfers between devices with their start and end apart: 4 -> 0, of which waited for: 4 -> 0; matrix products, arithmetic and copies ran while one was open for 6% -> 0% of each run, Pallas kernels for 0% -> 0%
where the time goes in v1:
time: 60.2 us; the launch traced here: 59.9 us
  Pallas kernels  52.5 us (87%)
  local copies, waits for them, and re-layouts  6.8 us (11%)
  between operations  0.65 us (1%)
    pallas_call x1, Pallas kernels, fused_on_device(): pl.pallas_call(functools.partial(fused, n_blk, n_grp, hd), out_shape=[jax...  52.5 us
    unnamed x13, local copies, waits for them, and re-layouts  6.8 us

profile of v1, /device:TPU:0, one launch (start us, length us, event | category | flops | bytes accessed | tf_op | source)
XLA Modules:
  0.0 59.9 jit_solution(12616189805381749188)
XLA Ops:
  0.6 0.0 copy-start
  0.6 1.1 %copy-done = bf16[256,1536]{1,0:T(8,128)(2,1)S(1)} copy-done((bf16[256,1536]{1,0:T(8,128)(2,1)S(1)}, bf16[256,1536]{1,0:T(8,128)(2,1)}, u32[]{:S(2)}) %copy-start) | copy-done | bytes 786456
  1.8 0.0 copy-start.1
  1.8 1.1 %copy-done.1 = bf16[256,1536]{1,0:T(8,128)(2,1)S(1)} copy-done((bf16[256,1536]{1,0:T(8,128)(2,1)S(1)}, bf16[256,1536]{1,0:T(8,128)(2,1)}, u32[]{:S(2)}) %copy-start.1) | copy-done | bytes 786456
  2.9 0.0 copy-start.2
  2.9 0.9 %copy-done.2 = bf16[64,1536]{1,0:T(8,128)(2,1)S(1)} copy-done((bf16[64,1536]{1,0:T(8,128)(2,1)S(1)}, bf16[64,1536]{1,0:T(8,128)(2,1)}, u32[]{:S(2)}) %copy-start.2) | copy-done | bytes 196632
  3.8 0.0 copy-start.3
  3.8 0.9 %copy-done.3 = bf16[64,1536]{1,0:T(8,128)(2,1)S(1)} copy-done((bf16[64,1536]{1,0:T(8,128)(2,1)S(1)}, bf16[64,1536]{1,0:T(8,128)(2,1)}, u32[]{:S(2)}) %copy-start.3) | copy-done | bytes 196632
  4.8 0.0 copy-start.4
  4.8 0.7 %copy-done.4 = s32[128]{0:T(128)S(1)} copy-done((s32[128]{0:T(128)S(1)}, s32[128]{0:T(128)}, u32[]{:S(2)}) %copy-start.4) | copy-done | bytes 536
  5.4 52.5 %shard_map.76 = (bf16[64,1536]{1,0:T(8,128)(2,1)S(1)}, bf16[64,1536]{1,0:T(8,128)(2,1)S(1)}, bf16[64,1536]{1,0:T(8,128)(2,1)S(1)}) custom-call(bf16[64,1536]{1,0:T(8,128)(2,1)S(1)} %copy-done.2, bf16[64,1536]{1,0:T(8,128)(2,1)S(1)} %copy-done.3, bf16[256,1536]{1,0:T(8,128)(2,1)S(1)} %copy-done, bf16[256,1536]{1,0:T(8,128)(2,1)S(1)} %copy-done.1, ...), custom_call_target="tpu_custom_call" | custom-call | tf_op jit(solution)/shard_map/pallas_call | solution.py:442
  57.9 0.7 %copy.11 = bf16[64,1536]{1,0:T(8,128)(2,1)} copy(bf16[64,1536]{1,0:T(8,128)(2,1)S(1)} %get-tuple-element.6) | data formatting | bytes 393216
  58.6 0.7 %copy.12 = bf16[64,1536]{1,0:T(8,128)(2,1)} copy(bf16[64,1536]{1,0:T(8,128)(2,1)S(1)} %get-tuple-element.7) | data formatting | bytes 393216
  59.2 0.7 %copy.13 = bf16[64,1536]{1,0:T(8,128)(2,1)} copy(bf16[64,1536]{1,0:T(8,128)(2,1)S(1)} %get-tuple-element.8) | data formatting | bytes 393216
Async XLA Ops:
  0.6 1.1 %copy-start = (bf16[256,1536]{1,0:T(8,128)(2,1)S(1)}, bf16[256,1536]{1,0:T(8,128)(2,1)}, u32[]{:S(2)}) copy-start(bf16[256,1536]{1,0:T(8,128)(2,1)} %k_ref.1) | copy-start | bytes 2359300
  1.8 1.1 %copy-start.1 = (bf16[256,1536]{1,0:T(8,128)(2,1)S(1)}, bf16[256,1536]{1,0:T(8,128)(2,1)}, u32[]{:S(2)}) copy-start(bf16[256,1536]{1,0:T(8,128)(2,1)} %v_ref.1) | copy-start | bytes 2359300
  2.9 0.9 %copy-start.2 = (bf16[64,1536]{1,0:T(8,128)(2,1)S(1)}, bf16[64,1536]{1,0:T(8,128)(2,1)}, u32[]{:S(2)}) copy-start(bf16[64,1536]{1,0:T(8,128)(2,1)} %q_ref.1) | copy-start | bytes 589828
  3.8 0.9 %copy-start.3 = (bf16[64,1536]{1,0:T(8,128)(2,1)S(1)}, bf16[64,1536]{1,0:T(8,128)(2,1)}, u32[]{:S(2)}) copy-start(bf16[64,1536]{1,0:T(8,128)(2,1)} %g_ref.1) | copy-start | bytes 589828
  4.8 0.7 %copy-start.4 = (s32[128]{0:T(128)S(1)}, s32[128]{0:T(128)}, u32[]{:S(2)}) copy-start(s32[128]{0:T(128)} %order_ref.1) | copy-start | bytes 1540

commit v2 on v0

--- a/solution.py
+++ b/solution.py
@@ -1,8 +1,11 @@
+import functools
 import math
 
 import jax
 import jax.numpy as jnp
 from jax import lax
+from jax.experimental import pallas as pl
+from jax.experimental.pallas import tpu as pltpu
 from jax.sharding import PartitionSpec as P
 
 H = 16
@@ -154,6 +157,377 @@
     return (query_total.astype(jnp.bfloat16), key_grad, value_grad)
 
 
+MESH = pl.DeviceIdType.MESH
+F32 = jnp.float32
+BF16 = jnp.bfloat16
+
+
+def mm(a, b, ca, cb):
+    return lax.dot_general(a, b, (((ca,), (cb,)), ((), ())), preferred_element_type=F32)
+
+
+def turn(x):
+    return x.T
+
+
+def fused(
+    n_blk,
+    n_grp,
+    hd,
+    q_ref,
+    g_ref,
+    k_ref,
+    v_ref,
+    order_ref,
+    oq_ref,
+    ok_ref,
+    ov_ref,
+    kv_in,
+    kvt_own,
+    kvt,
+    qz,
+    qgt_own,
+    qgt,
+    s_buf,
+    d_buf,
+    probs,
+    qst,
+    full_q,
+    pair_st,
+    pair_rv,
+    own_st,
+    full_kv,
+    onehot,
+    zst,
+    l_s,
+    kv_ss,
+    kv_rs,
+    fw_ss,
+    fw_rs,
+    z_ss,
+    z_rs,
+    q_ss,
+    q_rs,
+    b_ss,
+    b_rs,
+    p_ss,
+    p_rs,
+    d_ss,
+    d_rs,
+    o_ss,
+    o_rs,
+):
+    b = lax.axis_index("blk")
+    g = lax.axis_index("grp")
+    chips = n_grp // 2
+    p = g // 2
+    c = g % 2
+    partner = 2 * p + 1 - c
+    rows = q_ref.shape[0]
+    cols = k_ref.shape[0]
+    gw = chips * hd
+    scaling = 1.0 / math.sqrt(hd)
+    expc = scaling * math.log2(math.e)
+
+    def lanes(index, width):
+        return pl.ds(pl.multiple_of(index * width, width), width)
+
+    def describe(src, dst, ss, rs, bb, gg):
+        return pltpu.make_async_remote_copy(
+            src_ref=src,
+            dst_ref=dst,
+            send_sem=ss,
+            recv_sem=rs,
+            device_id=(bb, gg),
+            device_id_type=MESH,
+        )
+
+    started = []
+
+    def remote(*args):
+        copy = describe(*args)
+        copy.start()
+        started.append(copy)
+        return copy
+
+    local = []
+    for t, ref in enumerate((k_ref, v_ref)):
+        local.append(pltpu.make_async_copy(ref.at[:, lanes(b, gw)], kv_in.at[t], l_s.at[t]))
+    for t, ref in enumerate((q_ref, g_ref)):
+        local.append(
+            pltpu.make_async_copy(
+                ref.at[:, lanes(b, gw)], qz.at[t, lanes(b, rows), :], l_s.at[2 + t]
+            )
+        )
+    for copy in local:
+        copy.start()
+
+    barrier = pltpu.get_barrier_semaphore()
+    for d in range(1, n_blk):
+        pl.semaphore_signal(barrier, inc=1, device_id=((b + d) % n_blk, g), device_id_type=MESH)
+    for e in range(1, chips):
+        pl.semaphore_signal(
+            barrier, inc=1, device_id=(b, 2 * ((p + e) % chips) + c), device_id_type=MESH
+        )
+    pl.semaphore_signal(barrier, inc=1, device_id=(b, partner), device_id_type=MESH)
+
+    for t in range(2):
+        local[t].wait()
+        part = turn(kv_in[t])
+        for hl in range(chips):
+            kvt_own[hl, t] = part[hd * hl : hd * hl + hd]
+    pl.semaphore_wait(barrier, n_blk + chips - 1)
+
+    z_copies = {}
+    for t, ref in enumerate((q_ref, g_ref)):
+        for d in range(1, n_blk):
+            bb = (b + d) % n_blk
+            z_copies[t, d] = remote(
+                ref.at[:, lanes(bb, gw)],
+                qz.at[t, lanes(b, rows), :],
+                z_ss.at[d - 1, t],
+                z_rs.at[d - 1, t],
+                bb,
+                g,
+            )
+    kv_copies = {}
+    for e in range(1, chips):
+        pp = (p + e) % chips
+        kv_copies[e] = remote(
+            kvt_own.at[pp], kvt.at[g], kv_ss.at[e - 1], kv_rs.at[e - 1], b, 2 * pp + c
+        )
+    forwards = [remote(kvt_own.at[p], kvt.at[g], fw_ss.at[0], fw_rs.at[0], b, partner)]
+    kvt[g] = kvt_own[p]
+
+    row = lax.broadcasted_iota(jnp.int32, (PENCIL, cols), 0)
+    col = lax.broadcasted_iota(jnp.int32, (PENCIL, cols), 1)
+    per = rows // PENCIL
+    for bb in range(n_blk):
+        for k in range(per):
+            first = order_ref[(bb * n_grp + g) * per + k] * PENCIL - g * cols
+            onehot[pl.ds(bb * rows + k * PENCIL, PENCIL), :] = jnp.where(
+                col - row == first, 1.0, 0.0
+            ).astype(BF16)
+
+    for t in range(2):
+        local[2 + t].wait()
+        for d in range(1, n_blk):
+            z_copies[t, d].wait_recv()
+        part = turn(qz[t])
+        for hl in range(chips):
+            qgt_own[hl, t] = part[hd * hl : hd * hl + hd]
+        for e in range(1, chips):
+            pp = (p + e) % chips
+            remote(
+                qgt_own.at[pp, t],
+                qgt.at[p, t],
+                q_ss.at[e - 1, t],
+                q_rs.at[e - 1, t],
+                b,
+                2 * pp + c,
+            )
+        qgt[p, t] = qgt_own[p, t]
+        if t == 0:
+            for e in range(1, chips):
+                src = 2 * ((p - e + chips) % chips) + c
+                kv_copies[e].wait_recv()
+                forwards.append(
+                    remote(kvt.at[src], kvt.at[src], fw_ss.at[e], fw_rs.at[e], b, partner)
+                )
+    for copy in forwards:
+        copy.wait_recv()
+
+    def back(e, src):
+        return describe(
+            qst.at[e], full_q.at[p], b_ss.at[e - 1], b_rs.at[e - 1], b, 2 * src + c
+        )
+
+    def block(e, carry):
+        src = (p - e + chips) % chips
+
+        @pl.when(e > 0)
+        def _():
+            for t in range(2):
+                describe(
+                    qgt_own.at[0, t],
+                    qgt.at[src, t],
+                    q_ss.at[e - 1, t],
+                    q_rs.at[e - 1, t],
+                    b,
+                    2 * src + c,
+                ).wait_recv()
+
+        qb = turn(qgt[src, 0])
+        gb = turn(qgt[src, 1])
+        top = jnp.full((cols, cols), -jnp.inf, F32)
+        for n in range(n_grp):
+            s = mm(qb, kvt[n, 0], 1, 0)
+            s_buf[n] = s
+            top = jnp.maximum(top, s)
+        top = jnp.max(top, axis=1, keepdims=True)
+        tot = jnp.zeros((cols, cols), F32)
+        wtd = jnp.zeros((cols, cols), F32)
+        for n in range(n_grp):
+            x = jnp.exp2((s_buf[n] - top) * expc)
+            dp = mm(gb, kvt[n, 1], 1, 0)
+            s_buf[n] = x
+            d_buf[n] = dp
+            tot = tot + x
+            wtd = wtd + x * dp
+        inv = 1.0 / jnp.sum(tot, axis=1, keepdims=True)
+        mean = jnp.sum(wtd, axis=1, keepdims=True) * inv
+        acc = jnp.zeros((cols, hd), F32)
+        for n in range(n_grp):
+            soft = s_buf[n] * inv
+            sg = (scaling * soft * (d_buf[n] - mean)).astype(BF16)
+            probs[e, 0, n] = sg
+            probs[e, 1, n] = soft.astype(BF16)
+            acc = acc + mm(sg, kvt[n, 0], 1, 1)
+        qst[e] = turn(acc).astype(BF16)
+
+        @pl.when(e > 0)
+        def _():
+            back(e, src).start()
+
+        return carry
+
+    lax.fori_loop(0, chips, block, 0)
+    full_q[p] = qst[0]
+
+    def sums(t, n):
+        total = mm(qgt[p, t], probs[0, t, n], 1, 0)
+        for e in range(1, chips):
+            total = total + mm(qgt[(p - e + chips) % chips, t], probs[e, t, n], 1, 0)
+        return total
+
+    order = [*range(1, chips), 0]
+    pair = {}
+    for t in range(2):
+        for e in order:
+            pair_st[e, t] = sums(t, 2 * ((p + e) % chips) + 1 - c).astype(BF16)
+            pair[e, t] = remote(
+                pair_st.at[e, t], pair_rv.at[e, t], p_ss.at[e, t], p_rs.at[e, t], b, partner
+            )
+
+    out_copies = []
+
+    def deliver(t, value, out):
+        zst[t] = value
+        for d in range(1, n_blk):
+            bb = (b + d) % n_blk
+            out_copies.append(
+                remote(
+                    zst.at[t, lanes(bb, rows), :],
+                    out.at[:, lanes(b, gw)],
+                    o_ss.at[d - 1, t],
+                    o_rs.at[d - 1, t],
+                    bb,
+                    g,
+                )
+            )
+        out[:, lanes(b, gw)] = zst[t, lanes(b, rows), :]
+
+    home = {}
+
+    def finish(t):
+        for e in order:
+            pp = (p + e) % chips
+            mine = sums(t, 2 * pp + c)
+            pair[e, t].wait_recv()
+            done = (mine + pair_rv[e, t].astype(F32)).astype(BF16)
+            if e:
+                own_st[e - 1, t] = done
+                home[e, t] = remote(
+                    own_st.at[e - 1, t],
+                    full_kv.at[p, t],
+                    d_ss.at[e - 1, t],
+                    d_rs.at[e - 1, t],
+                    b,
+                    2 * pp + c,
+                )
+            else:
+                full_kv[p, t] = done
+
+    def permuted(t, out):
+        for e in range(1, chips):
+            home[e, t].wait_recv()
+        both = full_kv[:, t].reshape(gw, cols)
+        deliver(1 + t, mm(onehot[...], both, 1, 1).astype(BF16), out)
+
+    finish(0)
+    for e in range(1, chips):
+        back(e, (p - e + chips) % chips).wait_recv()
+    deliver(0, turn(full_q[...].reshape(gw, cols)), oq_ref)
+    finish(1)
+    permuted(0, ok_ref)
+    permuted(1, ov_ref)
+
+    for copy in out_copies:
+        copy.wait_recv()
+    for copy in started:
+        copy.wait_send()
+    for e in range(1, chips):
+        back(e, (p - e + chips) % chips).wait_send()
+
+
+def fused_on_device(n_blk, n_grp, obj_query, grad_out, pattern_key, pattern_value, pencil_order):
+    rows, features = obj_query.shape
+    cols = pattern_key.shape[0]
+    hd = features // H
+    chips = n_grp // 2
+    gw = chips * hd
+    dma = pltpu.SemaphoreType.DMA
+    vmem = pl.BlockSpec(memory_space=pltpu.VMEM)
+    anywhere = pl.BlockSpec(memory_space=pltpu.HBM)
+    return tuple(
+        pl.pallas_call(
+            functools.partial(fused, n_blk, n_grp, hd),
+            out_shape=[jax.ShapeDtypeStruct((rows, features), BF16)] * 3,
+            in_specs=[anywhere] * 4 + [pl.BlockSpec(memory_space=pltpu.SMEM)],
+            out_specs=[vmem] * 3,
+            scratch_shapes=[
+                pltpu.VMEM((2, cols, gw), BF16),
+                pltpu.VMEM((chips, 2, hd, cols), BF16),
+                pltpu.VMEM((n_grp, 2, hd, cols), BF16),
+                pltpu.VMEM((2, cols, gw), BF16),
+                pltpu.VMEM((chips, 2, hd, cols), BF16),
+                pltpu.VMEM((chips, 2, hd, cols), BF16),
+                pltpu.VMEM((n_grp, cols, cols), F32),
+                pltpu.VMEM((n_grp, cols, cols), F32),
+                pltpu.VMEM((chips, 2, n_grp, cols, cols), BF16),
+                pltpu.VMEM((chips, hd, cols), BF16),
+                pltpu.VMEM((chips, hd, cols), BF16),
+                pltpu.VMEM((chips, 2, hd, cols), BF16),
+                pltpu.VMEM((chips, 2, hd, cols), BF16),
+                pltpu.VMEM((chips - 1, 2, hd, cols), BF16),
+                pltpu.VMEM((chips, 2, hd, cols), BF16),
+                pltpu.VMEM((cols, cols), BF16),
+                pltpu.VMEM((3, cols, gw), BF16),
+                dma((4,)),
+                dma((chips - 1,)),
+                dma((chips - 1,)),
+                dma((chips,)),
+                dma((chips,)),
+                dma((n_blk - 1, 2)),
+                dma((n_blk - 1, 2)),
+                dma((chips - 1, 2)),
+                dma((chips - 1, 2)),
+                dma((chips - 1,)),
+                dma((chips - 1,)),
+                dma((chips, 2)),
+                dma((chips, 2)),
+                dma((chips - 1, 2)),
+                dma((chips - 1, 2)),
+                dma((n_blk - 1, 3)),
+                dma((n_blk - 1, 3)),
+            ],
+            compiler_params=pltpu.CompilerParams(
+                collective_id=0, has_side_effects=True, vmem_limit_bytes=56 * 1024 * 1024
+            ),
+        )(obj_query, grad_out, pattern_key, pattern_value, pencil_order)
+    )
+
+
 def solution(mesh):
     in_specs = (
         P(("blk", "grp"), None),
@@ -163,6 +537,17 @@
         P(),
     )
     out_specs = (P(("blk", "grp"), None), P(("blk", "grp"), None), P(("blk", "grp"), None))
-    return jax.shard_map(
-        on_device, mesh=mesh, in_specs=in_specs, out_specs=out_specs, check_vma=False
-    )
+    n_blk, n_grp = mesh.shape["blk"], mesh.shape["grp"]
+
+    def body(obj_query, grad_out, pattern_key, pattern_value, pencil_order):
+        features = obj_query.shape[1]
+        fits = (
+            n_blk * n_grp // 2 == H
+            and (features // n_blk) % 128 == 0
+            and pattern_key.shape[0] == 256
+            and n_blk * obj_query.shape[0] == 256
+        )
+        step = functools.partial(fused_on_device, n_blk, n_grp) if fits else on_device
+        return step(obj_query, grad_out, pattern_key, pattern_value, pencil_order)
+
+    return jax.shard_map(body, mesh=mesh, in_specs=in_specs, out_specs=out_specs, check_vma=False)

time: 299 us -> 48.6 us (0.16)
  waiting for transfers between devices: 148 us -> 0 us
  local copies, waits for them, and re-layouts: 53.3 us -> 3.33 us
  Pallas kernels: 0 us -> 44.4 us
  matrix products: 31.2 us -> 0 us
  blocking collectives: 26.9 us -> 0 us
  other arithmetic: 22.8 us -> 0 us
  between operations: 14 us -> 0.65 us
    reduce_scatter x2 -> x0, waiting for transfers between devices: 94 us -> none  [the longest x1 60.9 us: on_device(): lax.psum_scatter(jnp.concatenate([jnp.take(keys_acc, source, axis=0), jnp...]
    all_gather x2 -> x0, waiting for transfers between devices: 52.9 us -> none  [the longest x1 27.9 us: on_device(): lax.all_gather(obj_query, 'grp', axis=0, tiled=True)]
    pallas_call x0 -> x1, Pallas kernels: none -> 44.4 us  [fused_on_device(): pl.pallas_call(functools.partial(fused, n_blk, n_grp, hd), out_shape=[jax...]
    dot_general x28 -> x0, matrix products: 31.2 us -> none  [the longest x4 5.92 us: block_grads(): jnp.einsum('hrc,rhd->chd', score_grad, query_heads, preferred_element_typ...]
    all_gather x3 -> x0, blocking collectives: 26.9 us -> none  [joined(): everything = jax.tree.map(lambda part: lax.all_gather(part, axis), value)]
    dynamic_slice x24 -> x0, local copies, waits for them, and re-layouts: 20.5 us -> none  [the longest x16 20.4 us: stats_of_rows(): lax.map(one_block, (queries.reshape(amount // blocking, blocking, feature...]
    dynamic_update_slice x16 -> x0, local copies, waits for them, and re-layouts: 13 us -> none  [the longest x8 12.9 us: on_device(): lax.scan(sweep, (zeros_acc, zeros_acc), segments)]
    add x18 -> x0, other arithmetic: 12.9 us -> none  [the longest x4 12.4 us: sweep(): return ((keys_acc + key_term, values_acc + value_term), query_term)]
  transfers between devices with their start and end apart: 4 -> 0, of which waited for: 4 -> 0; matrix products, arithmetic and copies ran while one was open for 6% -> 0% of each run, Pallas kernels for 0% -> 0%
where the time goes in v2:
time: 48.6 us; the launch traced here: 48.4 us
  Pallas kernels  44.4 us (91%)
  local copies, waits for them, and re-layouts  3.33 us (7%)
  between operations  0.65 us (1%)
    pallas_call x1, Pallas kernels, fused_on_device(): pl.pallas_call(functools.partial(fused, n_blk, n_grp, hd), out_shape=[jax...  44.4 us
    unnamed x7, local copies, waits for them, and re-layouts  3.33 us

profile of v2, /device:TPU:0, one launch (start us, length us, event | category | flops | bytes accessed | tf_op | source)
XLA Modules:
  0.0 48.4 jit_solution(14704690838832761390)
XLA Ops:
  0.6 44.4 %shard_map.76 = (bf16[64,1536]{1,0:T(8,128)(2,1)}, bf16[64,1536]{1,0:T(8,128)(2,1)}, bf16[64,1536]{1,0:T(8,128)(2,1)}) custom-call(bf16[64,1536]{1,0:T(8,128)(2,1)} %q_ref.1, bf16[64,1536]{1,0:T(8,128)(2,1)} %g_ref.1, bf16[256,1536]{1,0:T(8,128)(2,1)} %k_ref.1, bf16[256,1536]{1,0:T(8,128)(2,1)} %v_ref.1, s32[128]{0:T(128)} %order_ref.1), custom_call_target="tpu_custom_call" | custom-call | tf_op jit(solution)/shard_map/pallas_call | solution.py:483
  45.1 0.0 copy-start.1
  45.1 1.7 %copy.11 = bf16[64,1536]{1,0:T(8,128)(2,1)} copy(bf16[64,1536]{1,0:T(8,128)(2,1)} %get-tuple-element.6) | data formatting | bytes 393216
  46.7 0.0 copy-done.1
  46.7 0.0 copy-start
  46.7 0.7 %copy.12 = bf16[64,1536]{1,0:T(8,128)(2,1)} copy(bf16[64,1536]{1,0:T(8,128)(2,1)S(1)} %copy-done.1) | data formatting | bytes 393216
  47.4 0.3 copy-done
  47.7 0.7 %copy.13 = bf16[64,1536]{1,0:T(8,128)(2,1)} copy(bf16[64,1536]{1,0:T(8,128)(2,1)S(1)} %copy-done) | data formatting | bytes 393216
Async XLA Ops:
  45.1 1.7 %copy-start.1 = (bf16[64,1536]{1,0:T(8,128)(2,1)S(1)}, bf16[64,1536]{1,0:T(8,128)(2,1)}, u32[]{:S(2)}) copy-start(bf16[64,1536]{1,0:T(8,128)(2,1)} %get-tuple-element.7) | copy-start | bytes 589828
  46.7 1.0 %copy-start = (bf16[64,1536]{1,0:T(8,128)(2,1)S(1)}, bf16[64,1536]{1,0:T(8,128)(2,1)}, u32[]{:S(2)}) copy-start(bf16[64,1536]{1,0:T(8,128)(2,1)} %get-tuple-element.8) | copy-start | bytes 589828

commit v3 on v2

--- a/solution.py
+++ b/solution.py
@@ -190,7 +190,8 @@
     qgt,
     s_buf,
     d_buf,
-    probs,
+    inv_buf,
+    kvacc,
     qst,
     full_q,
     pair_st,
@@ -279,6 +280,8 @@
     pl.semaphore_wait(barrier, n_blk + chips - 1)
 
     z_copies = {}
+    kv_copies = {}
+    forwards = {}
     for t, ref in enumerate((q_ref, g_ref)):
         for d in range(1, n_blk):
             bb = (b + d) % n_blk
@@ -290,14 +293,21 @@
                 bb,
                 g,
             )
-    kv_copies = {}
-    for e in range(1, chips):
-        pp = (p + e) % chips
-        kv_copies[e] = remote(
-            kvt_own.at[pp], kvt.at[g], kv_ss.at[e - 1], kv_rs.at[e - 1], b, 2 * pp + c
-        )
-    forwards = [remote(kvt_own.at[p], kvt.at[g], fw_ss.at[0], fw_rs.at[0], b, partner)]
+        for e in range(1, chips):
+            pp = (p + e) % chips
+            kv_copies[t, e] = remote(
+                kvt_own.at[pp, t],
+                kvt.at[g, t],
+                kv_ss.at[e - 1, t],
+                kv_rs.at[e - 1, t],
+                b,
+                2 * pp + c,
+            )
+        forwards[t, 0] = remote(
+            kvt_own.at[p, t], kvt.at[g, t], fw_ss.at[0, t], fw_rs.at[0, t], b, partner
+        )
     kvt[g] = kvt_own[p]
+    kvacc[...] = jnp.zeros_like(kvacc)
 
     row = lax.broadcasted_iota(jnp.int32, (PENCIL, cols), 0)
     col = lax.broadcasted_iota(jnp.int32, (PENCIL, cols), 1)
@@ -309,7 +319,15 @@
                 col - row == first, 1.0, 0.0
             ).astype(BF16)
 
-    for t in range(2):
+    def forward(t):
+        for e in range(1, chips):
+            src = 2 * ((p - e + chips) % chips) + c
+            kv_copies[t, e].wait_recv()
+            forwards[t, e] = remote(
+                kvt.at[src, t], kvt.at[src, t], fw_ss.at[e, t], fw_rs.at[e, t], b, partner
+            )
+
+    def exchange(t):
         local[2 + t].wait()
         for d in range(1, n_blk):
             z_copies[t, d].wait_recv()
@@ -327,61 +345,70 @@
                 2 * pp + c,
             )
         qgt[p, t] = qgt_own[p, t]
-        if t == 0:
-            for e in range(1, chips):
-                src = 2 * ((p - e + chips) % chips) + c
-                kv_copies[e].wait_recv()
-                forwards.append(
-                    remote(kvt.at[src], kvt.at[src], fw_ss.at[e], fw_rs.at[e], b, partner)
-                )
-    for copy in forwards:
-        copy.wait_recv()
+
+    def arrived(t, e, src):
+        describe(
+            qgt_own.at[0, t],
+            qgt.at[src, t],
+            q_ss.at[e - 1, t],
+            q_rs.at[e - 1, t],
+            b,
+            2 * src + c,
+        ).wait_recv()
+
+    def from_chip(e):
+        return (p - e + chips) % chips
 
     def back(e, src):
         return describe(
             qst.at[e], full_q.at[p], b_ss.at[e - 1], b_rs.at[e - 1], b, 2 * src + c
         )
 
-    def block(e, carry):
-        src = (p - e + chips) % chips
+    def weights(e, carry):
+        src = from_chip(e)
 
         @pl.when(e > 0)
         def _():
-            for t in range(2):
-                describe(
-                    qgt_own.at[0, t],
-                    qgt.at[src, t],
-                    q_ss.at[e - 1, t],
-                    q_rs.at[e - 1, t],
-                    b,
-                    2 * src + c,
-                ).wait_recv()
+            arrived(0, e, src)
 
         qb = turn(qgt[src, 0])
-        gb = turn(qgt[src, 1])
         top = jnp.full((cols, cols), -jnp.inf, F32)
         for n in range(n_grp):
             s = mm(qb, kvt[n, 0], 1, 0)
-            s_buf[n] = s
+            s_buf[e, n] = s
             top = jnp.maximum(top, s)
         top = jnp.max(top, axis=1, keepdims=True)
         tot = jnp.zeros((cols, cols), F32)
+        for n in range(n_grp):
+            x = jnp.exp2((s_buf[e, n] - top) * expc)
+            s_buf[e, n] = x
+            tot = tot + x
+        inv_buf[e] = 1.0 / jnp.sum(tot, axis=1, keepdims=True)
+        return carry
+
+    def value_sums(n):
+        total = jnp.zeros((hd, cols), F32)
+        for e in range(chips):
+            low = (s_buf[e, n] * inv_buf[e]).astype(BF16)
+            total = total + mm(qgt[from_chip(e), 1], low, 1, 0)
+        return total
+
+    def grads(e, carry):
+        src = from_chip(e)
+        qt = qgt[src, 0]
+        gb = turn(qgt[src, 1])
         wtd = jnp.zeros((cols, cols), F32)
         for n in range(n_grp):
-            x = jnp.exp2((s_buf[n] - top) * expc)
             dp = mm(gb, kvt[n, 1], 1, 0)
-            s_buf[n] = x
             d_buf[n] = dp
-            tot = tot + x
-            wtd = wtd + x * dp
-        inv = 1.0 / jnp.sum(tot, axis=1, keepdims=True)
+            wtd = wtd + s_buf[e, n] * dp
+        inv = inv_buf[e]
         mean = jnp.sum(wtd, axis=1, keepdims=True) * inv
         acc = jnp.zeros((cols, hd), F32)
         for n in range(n_grp):
-            soft = s_buf[n] * inv
+            soft = s_buf[e, n] * inv
             sg = (scaling * soft * (d_buf[n] - mean)).astype(BF16)
-            probs[e, 0, n] = sg
-            probs[e, 1, n] = soft.astype(BF16)
+            kvacc[0, n] += mm(qt, sg, 1, 0)
             acc = acc + mm(sg, kvt[n, 0], 1, 1)
         qst[e] = turn(acc).astype(BF16)
 
@@ -391,23 +418,33 @@
 
         return carry
 
-    lax.fori_loop(0, chips, block, 0)
-    full_q[p] = qst[0]
-
-    def sums(t, n):
-        total = mm(qgt[p, t], probs[0, t, n], 1, 0)
-        for e in range(1, chips):
-            total = total + mm(qgt[(p - e + chips) % chips, t], probs[e, t, n], 1, 0)
-        return total
-
     order = [*range(1, chips), 0]
     pair = {}
-    for t in range(2):
-        for e in order:
-            pair_st[e, t] = sums(t, 2 * ((p + e) % chips) + 1 - c).astype(BF16)
-            pair[e, t] = remote(
-                pair_st.at[e, t], pair_rv.at[e, t], p_ss.at[e, t], p_rs.at[e, t], b, partner
-            )
+
+    def swap(t, e, total):
+        pair_st[e, t] = total.astype(BF16)
+        pair[e, t] = remote(
+            pair_st.at[e, t], pair_rv.at[e, t], p_ss.at[e, t], p_rs.at[e, t], b, partner
+        )
+
+    forward(0)
+    exchange(0)
+    for e in range(chips):
+        forwards[0, e].wait_recv()
+    lax.fori_loop(0, 2, weights, 0)
+    forward(1)
+    exchange(1)
+    lax.fori_loop(2, chips, weights, 0)
+    for e in range(1, chips):
+        arrived(1, e, from_chip(e))
+    for e in order:
+        swap(1, e, value_sums(2 * ((p + e) % chips) + 1 - c))
+    for e in order:
+        n = 2 * ((p + e) % chips) + c
+        kvacc[1, n] = value_sums(n)
+    for e in range(chips):
+        forwards[1, e].wait_recv()
+    lax.fori_loop(0, 2, grads, 0)
 
     out_copies = []
 
@@ -432,7 +469,7 @@
     def finish(t):
         for e in order:
             pp = (p + e) % chips
-            mine = sums(t, 2 * pp + c)
+            mine = kvacc[t, 2 * pp + c]
             pair[e, t].wait_recv()
             done = (mine + pair_rv[e, t].astype(F32)).astype(BF16)
             if e:
@@ -454,20 +491,24 @@
         both = full_kv[:, t].reshape(gw, cols)
         deliver(1 + t, mm(onehot[...], both, 1, 1).astype(BF16), out)
 
+    finish(1)
+    lax.fori_loop(2, chips, grads, 0)
+    full_q[p] = qst[0]
+    for e in order:
+        swap(0, e, kvacc[0, 2 * ((p + e) % chips) + 1 - c])
+    permuted(1, ov_ref)
+    for e in range(1, chips):
+        back(e, from_chip(e)).wait_recv()
+    deliver(0, turn(full_q[...].reshape(gw, cols)), oq_ref)
     finish(0)
-    for e in range(1, chips):
-        back(e, (p - e + chips) % chips).wait_recv()
-    deliver(0, turn(full_q[...].reshape(gw, cols)), oq_ref)
-    finish(1)
     permuted(0, ok_ref)
-    permuted(1, ov_ref)
 
     for copy in out_copies:
         copy.wait_recv()
     for copy in started:
         copy.wait_send()
     for e in range(1, chips):
-        back(e, (p - e + chips) % chips).wait_send()
+        back(e, from_chip(e)).wait_send()
 
 
 def fused_on_device(n_blk, n_grp, obj_query, grad_out, pattern_key, pattern_value, pencil_order):
@@ -492,9 +533,10 @@
                 pltpu.VMEM((2, cols, gw), BF16),
                 pltpu.VMEM((chips, 2, hd, cols), BF16),
                 pltpu.VMEM((chips, 2, hd, cols), BF16),
+                pltpu.VMEM((chips, n_grp, cols, cols), F32),
                 pltpu.VMEM((n_grp, cols, cols), F32),
-                pltpu.VMEM((n_grp, cols, cols), F32),
-                pltpu.VMEM((chips, 2, n_grp, cols, cols), BF16),
+                pltpu.VMEM((chips, cols, 1), F32),
+                pltpu.VMEM((2, n_grp, hd, cols), F32),
                 pltpu.VMEM((chips, hd, cols), BF16),
                 pltpu.VMEM((chips, hd, cols), BF16),
                 pltpu.VMEM((chips, 2, hd, cols), BF16),
@@ -504,10 +546,10 @@
                 pltpu.VMEM((cols, cols), BF16),
                 pltpu.VMEM((3, cols, gw), BF16),
                 dma((4,)),
-                dma((chips - 1,)),
-                dma((chips - 1,)),
-                dma((chips,)),
-                dma((chips,)),
+                dma((chips - 1, 2)),
+                dma((chips - 1, 2)),
+                dma((chips, 2)),
+                dma((chips, 2)),
                 dma((n_blk - 1, 2)),
                 dma((n_blk - 1, 2)),
                 dma((chips - 1, 2)),

time: 48.6 us -> 50.3 us (1.035)
  Pallas kernels: 44.4 us -> 46.1 us
    pallas_call x1, Pallas kernels: 44.4 us -> 46.1 us  [fused_on_device(): pl.pallas_call(functools.partial(fused, n_blk, n_grp, hd), out_shape=[jax...]
where the time goes in v3:
time: 50.3 us; the launch traced here: 50.1 us
  Pallas kernels  46.1 us (92%)
  local copies, waits for them, and re-layouts  3.33 us (7%)
  between operations  0.65 us (1%)
    pallas_call x1, Pallas kernels, fused_on_device(): pl.pallas_call(functools.partial(fused, n_blk, n_grp, hd), out_shape=[jax...  46.1 us
    unnamed x7, local copies, waits for them, and re-layouts  3.33 us

profile of v3, /device:TPU:0, one launch (start us, length us, event | category | flops | bytes accessed | tf_op | source)
XLA Modules:
  0.0 50.1 jit_solution(3157647568092392229)
XLA Ops:
  0.6 46.1 %shard_map.76 = (bf16[64,1536]{1,0:T(8,128)(2,1)}, bf16[64,1536]{1,0:T(8,128)(2,1)}, bf16[64,1536]{1,0:T(8,128)(2,1)}) custom-call(bf16[64,1536]{1,0:T(8,128)(2,1)} %q_ref.1, bf16[64,1536]{1,0:T(8,128)(2,1)} %g_ref.1, bf16[256,1536]{1,0:T(8,128)(2,1)} %k_ref.1, bf16[256,1536]{1,0:T(8,128)(2,1)} %v_ref.1, s32[128]{0:T(128)} %order_ref.1), custom_call_target="tpu_custom_call" | custom-call | tf_op jit(solution)/shard_map/pallas_call | solution.py:524
  46.8 0.0 copy-start.1
  46.8 1.7 %copy.11 = bf16[64,1536]{1,0:T(8,128)(2,1)} copy(bf16[64,1536]{1,0:T(8,128)(2,1)} %get-tuple-element.6) | data formatting | bytes 393216
  48.4 0.0 copy-done.1
  48.4 0.0 copy-start
  48.4 0.7 %copy.12 = bf16[64,1536]{1,0:T(8,128)(2,1)} copy(bf16[64,1536]{1,0:T(8,128)(2,1)S(1)} %copy-done.1) | data formatting | bytes 393216
  49.1 0.3 copy-done
  49.4 0.7 %copy.13 = bf16[64,1536]{1,0:T(8,128)(2,1)} copy(bf16[64,1536]{1,0:T(8,128)(2,1)S(1)} %copy-done) | data formatting | bytes 393216
Async XLA Ops:
  46.8 1.7 %copy-start.1 = (bf16[64,1536]{1,0:T(8,128)(2,1)S(1)}, bf16[64,1536]{1,0:T(8,128)(2,1)}, u32[]{:S(2)}) copy-start(bf16[64,1536]{1,0:T(8,128)(2,1)} %get-tuple-element.7) | copy-start | bytes 589828
  48.4 1.0 %copy-start = (bf16[64,1536]{1,0:T(8,128)(2,1)S(1)}, bf16[64,1536]{1,0:T(8,128)(2,1)}, u32[]{:S(2)}) copy-start(bf16[64,1536]{1,0:T(8,128)(2,1)} %get-tuple-element.8) | copy-start | bytes 589828

commit v4 on v3

--- a/solution.py
+++ b/solution.py
@@ -179,9 +179,7 @@
     k_ref,
     v_ref,
     order_ref,
-    oq_ref,
-    ok_ref,
-    ov_ref,
+    out_ref,
     kv_in,
     kvt_own,
     kvt,
@@ -191,7 +189,8 @@
     s_buf,
     d_buf,
     inv_buf,
-    kvacc,
+    probs,
+    own_v,
     qst,
     full_q,
     pair_st,
@@ -272,11 +271,6 @@
         )
     pl.semaphore_signal(barrier, inc=1, device_id=(b, partner), device_id_type=MESH)
 
-    for t in range(2):
-        local[t].wait()
-        part = turn(kv_in[t])
-        for hl in range(chips):
-            kvt_own[hl, t] = part[hd * hl : hd * hl + hd]
     pl.semaphore_wait(barrier, n_blk + chips - 1)
 
     z_copies = {}
@@ -293,6 +287,11 @@
                 bb,
                 g,
             )
+    for t in range(2):
+        local[t].wait()
+        part = turn(kv_in[t])
+        for hl in range(chips):
+            kvt_own[hl, t] = part[hd * hl : hd * hl + hd]
         for e in range(1, chips):
             pp = (p + e) % chips
             kv_copies[t, e] = remote(
@@ -307,7 +306,6 @@
             kvt_own.at[p, t], kvt.at[g, t], fw_ss.at[0, t], fw_rs.at[0, t], b, partner
         )
     kvt[g] = kvt_own[p]
-    kvacc[...] = jnp.zeros_like(kvacc)
 
     row = lax.broadcasted_iota(jnp.int32, (PENCIL, cols), 0)
     col = lax.broadcasted_iota(jnp.int32, (PENCIL, cols), 1)
@@ -393,9 +391,14 @@
             total = total + mm(qgt[from_chip(e), 1], low, 1, 0)
         return total
 
+    def key_sums(n):
+        total = jnp.zeros((hd, cols), F32)
+        for e in range(chips):
+            total = total + mm(qgt[from_chip(e), 0], probs[e, n], 1, 0)
+        return total
+
     def grads(e, carry):
         src = from_chip(e)
-        qt = qgt[src, 0]
         gb = turn(qgt[src, 1])
         wtd = jnp.zeros((cols, cols), F32)
         for n in range(n_grp):
@@ -408,7 +411,7 @@
         for n in range(n_grp):
             soft = s_buf[e, n] * inv
             sg = (scaling * soft * (d_buf[n] - mean)).astype(BF16)
-            kvacc[0, n] += mm(qt, sg, 1, 0)
+            probs[e, n] = sg
             acc = acc + mm(sg, kvt[n, 0], 1, 1)
         qst[e] = turn(acc).astype(BF16)
 
@@ -440,36 +443,34 @@
     for e in order:
         swap(1, e, value_sums(2 * ((p + e) % chips) + 1 - c))
     for e in order:
-        n = 2 * ((p + e) % chips) + c
-        kvacc[1, n] = value_sums(n)
+        own_v[e] = value_sums(2 * ((p + e) % chips) + c)
     for e in range(chips):
         forwards[1, e].wait_recv()
-    lax.fori_loop(0, 2, grads, 0)
 
     out_copies = []
 
-    def deliver(t, value, out):
+    def deliver(t, value):
         zst[t] = value
         for d in range(1, n_blk):
             bb = (b + d) % n_blk
             out_copies.append(
                 remote(
                     zst.at[t, lanes(bb, rows), :],
-                    out.at[:, lanes(b, gw)],
+                    out_ref.at[t, :, lanes(b, gw)],
                     o_ss.at[d - 1, t],
                     o_rs.at[d - 1, t],
                     bb,
                     g,
                 )
             )
-        out[:, lanes(b, gw)] = zst[t, lanes(b, rows), :]
+        out_ref[t, :, lanes(b, gw)] = zst[t, lanes(b, rows), :]
 
     home = {}
 
     def finish(t):
         for e in order:
             pp = (p + e) % chips
-            mine = kvacc[t, 2 * pp + c]
+            mine = own_v[e] if t else key_sums(2 * pp + c)
             pair[e, t].wait_recv()
             done = (mine + pair_rv[e, t].astype(F32)).astype(BF16)
             if e:
@@ -485,23 +486,24 @@
             else:
                 full_kv[p, t] = done
 
-    def permuted(t, out):
+    def permuted(t):
         for e in range(1, chips):
             home[e, t].wait_recv()
         both = full_kv[:, t].reshape(gw, cols)
-        deliver(1 + t, mm(onehot[...], both, 1, 1).astype(BF16), out)
+        deliver(1 + t, mm(onehot[...], both, 1, 1).astype(BF16))
 
     finish(1)
+    lax.fori_loop(0, 2, grads, 0)
+    permuted(1)
     lax.fori_loop(2, chips, grads, 0)
     full_q[p] = qst[0]
     for e in order:
-        swap(0, e, kvacc[0, 2 * ((p + e) % chips) + 1 - c])
-    permuted(1, ov_ref)
+        swap(0, e, key_sums(2 * ((p + e) % chips) + 1 - c))
     for e in range(1, chips):
         back(e, from_chip(e)).wait_recv()
-    deliver(0, turn(full_q[...].reshape(gw, cols)), oq_ref)
+    deliver(0, turn(full_q[...].reshape(gw, cols)))
     finish(0)
-    permuted(0, ok_ref)
+    permuted(0)
 
     for copy in out_copies:
         copy.wait_recv()
@@ -520,12 +522,12 @@
     dma = pltpu.SemaphoreType.DMA
     vmem = pl.BlockSpec(memory_space=pltpu.VMEM)
     anywhere = pl.BlockSpec(memory_space=pltpu.HBM)
-    return tuple(
+    joined_out = (
         pl.pallas_call(
             functools.partial(fused, n_blk, n_grp, hd),
-            out_shape=[jax.ShapeDtypeStruct((rows, features), BF16)] * 3,
+            out_shape=jax.ShapeDtypeStruct((3, rows, features), BF16),
             in_specs=[anywhere] * 4 + [pl.BlockSpec(memory_space=pltpu.SMEM)],
-            out_specs=[vmem] * 3,
+            out_specs=vmem,
             scratch_shapes=[
                 pltpu.VMEM((2, cols, gw), BF16),
                 pltpu.VMEM((chips, 2, hd, cols), BF16),
@@ -536,7 +538,8 @@
                 pltpu.VMEM((chips, n_grp, cols, cols), F32),
                 pltpu.VMEM((n_grp, cols, cols), F32),
                 pltpu.VMEM((chips, cols, 1), F32),
-                pltpu.VMEM((2, n_grp, hd, cols), F32),
+                pltpu.VMEM((chips, n_grp, cols, cols), BF16),
+                pltpu.VMEM((chips, hd, cols), F32),
                 pltpu.VMEM((chips, hd, cols), BF16),
                 pltpu.VMEM((chips, hd, cols), BF16),
                 pltpu.VMEM((chips, 2, hd, cols), BF16),
@@ -568,6 +571,7 @@
             ),
         )(obj_query, grad_out, pattern_key, pattern_value, pencil_order)
     )
+    return joined_out[0], joined_out[1], joined_out[2]
 
 
 def solution(mesh):

time: 50.3 us -> 50.3 us (level)
  Pallas kernels: 46.1 us -> 47.5 us
  local copies, waits for them, and re-layouts: 3.33 us -> 1.94 us
    unnamed x7 -> x0, local copies, waits for them, and re-layouts: 3.33 us -> none
    squeeze x0 -> x1, local copies, waits for them, and re-layouts: none -> 1.94 us  [fused_on_device(): return (joined_out[0], joined_out[1], joined_out[2])]
    pallas_call x1, Pallas kernels: 46.1 us -> 47.5 us  [fused_on_device(): pl.pallas_call(functools.partial(fused, n_blk, n_grp, hd), out_shape=jax....]
where the time goes in v4:
time: 50.3 us; the launch traced here: 50.1 us
  Pallas kernels  47.5 us (94%)
  local copies, waits for them, and re-layouts  1.94 us (4%)
  between operations  0.64 us (1%)
    pallas_call x1, Pallas kernels, fused_on_device(): pl.pallas_call(functools.partial(fused, n_blk, n_grp, hd), out_shape=jax....  47.5 us
    squeeze x1, local copies, waits for them, and re-layouts, fused_on_device(): return (joined_out[0], joined_out[1], joined_out[2])  1.94 us

profile of v4, /device:TPU:0, one launch (start us, length us, event | category | flops | bytes accessed | tf_op | source)
XLA Modules:
  0.0 50.1 jit_solution(852063833764870088)
XLA Ops:
  0.6 47.5 %shard_map.76 = bf16[3,64,1536]{2,1,0:T(8,128)(2,1)} custom-call(bf16[64,1536]{1,0:T(8,128)(2,1)} %q_ref.1, bf16[64,1536]{1,0:T(8,128)(2,1)} %g_ref.1, bf16[256,1536]{1,0:T(8,128)(2,1)} %k_ref.1, bf16[256,1536]{1,0:T(8,128)(2,1)} %v_ref.1, s32[128]{0:T(128)} %order_ref.1), custom_call_target="tpu_custom_call" | custom-call | tf_op jit(solution)/shard_map/pallas_call | solution.py:526
  48.2 1.9 %slice_bitcast_fusion = (bf16[64,1536]{1,0:T(8,128)(2,1)}, bf16[64,1536]{1,0:T(8,128)(2,1)}, bf16[64,1536]{1,0:T(8,128)(2,1)}) fusion(bf16[3,64,1536]{2,1,0:T(8,128)(2,1)} %shard_map.76), kind=kLoop, calls=%fused_computation | loop fusion | bytes 1179648 | tf_op jit(solution)/shard_map/squeeze | solution.py:574

commit v5 on v4

--- a/solution.py
+++ b/solution.py
@@ -499,10 +499,10 @@
     full_q[p] = qst[0]
     for e in order:
         swap(0, e, key_sums(2 * ((p + e) % chips) + 1 - c))
+    finish(0)
     for e in range(1, chips):
         back(e, from_chip(e)).wait_recv()
     deliver(0, turn(full_q[...].reshape(gw, cols)))
-    finish(0)
     permuted(0)
 
     for copy in out_copies:

time: 50.3 us -> 48.9 us (0.972)
  Pallas kernels: 47.5 us -> 46.2 us
    pallas_call x1, Pallas kernels: 47.5 us -> 46.2 us  [fused_on_device(): pl.pallas_call(functools.partial(fused, n_blk, n_grp, hd), out_shape=jax....]
where the time goes in v5:
time: 48.9 us; the launch traced here: 48.7 us
  Pallas kernels  46.2 us (94%)
  local copies, waits for them, and re-layouts  1.94 us (4%)
  between operations  0.64 us (1%)
    pallas_call x1, Pallas kernels, fused_on_device(): pl.pallas_call(functools.partial(fused, n_blk, n_grp, hd), out_shape=jax....  46.2 us
    squeeze x1, local copies, waits for them, and re-layouts, fused_on_device(): return (joined_out[0], joined_out[1], joined_out[2])  1.94 us

profile of v5, /device:TPU:0, one launch (start us, length us, event | category | flops | bytes accessed | tf_op | source)
XLA Modules:
  0.0 48.7 jit_solution(5420285419616703435)
XLA Ops:
  0.6 46.2 %shard_map.76 = bf16[3,64,1536]{2,1,0:T(8,128)(2,1)} custom-call(bf16[64,1536]{1,0:T(8,128)(2,1)} %q_ref.1, bf16[64,1536]{1,0:T(8,128)(2,1)} %g_ref.1, bf16[256,1536]{1,0:T(8,128)(2,1)} %k_ref.1, bf16[256,1536]{1,0:T(8,128)(2,1)} %v_ref.1, s32[128]{0:T(128)} %order_ref.1), custom_call_target="tpu_custom_call" | custom-call | tf_op jit(solution)/shard_map/pallas_call | solution.py:526
  46.8 1.9 %slice_bitcast_fusion = (bf16[64,1536]{1,0:T(8,128)(2,1)}, bf16[64,1536]{1,0:T(8,128)(2,1)}, bf16[64,1536]{1,0:T(8,128)(2,1)}) fusion(bf16[3,64,1536]{2,1,0:T(8,128)(2,1)} %shard_map.76), kind=kLoop, calls=%fused_computation | loop fusion | bytes 1179648 | tf_op jit(solution)/shard_map/squeeze | solution.py:574
